TPU v7x, 32 devices: a whole 2x2x4 slice. The times are simulated.
32 devices in a mesh: pipe: 2 (over x), space: 16 (over z, y, core).
Axes of the slice: x: 2, y: 2, z: 4, core: 2. Of those that a mesh axis runs over, the one named last changes fastest.
Arguments:
- activations: bfloat16 [2, 2, 96, 256, 512], P('pipe', None, None, 'space'), may hold values from -6 to 6
- cotangent: bfloat16 [2, 2, 96, 256, 512], P('pipe', None, None, 'space'), may hold values from -6 to 6
- kept_modes: int32 [2, 2], P('pipe'), may hold values from 32 to 128, as said below
- weight_in: float32 [2, 2, 2, 96, 96], P('pipe'), may hold values from -0.4375 to 0.4375
- bias_in: float32 [2, 2, 2, 96], P('pipe'), may hold values from -4 to 4
- weight_out: float32 [2, 2, 2, 96, 96], P('pipe'), may hold values from -0.4375 to 0.4375
Outputs:
- grad_input: bfloat16 [2, 2, 96, 256, 512], P('pipe', None, None, 'space')
- grad_weight_in: float32 [2, 2, 2, 96, 96], P('pipe')
- grad_bias_in: float32 [2, 2, 2, 96], P('pipe')
- grad_weight_out: float32 [2, 2, 2, 96, 96], P('pipe')
- grad_bias_out: float32 [2, 2, 2, 96], P('pipe')
Inputs may be any that keep to these rules, and one draw needn't show every extreme that they name: `kept_modes`: column 0 is a layer's kept longitude wavenumbers, from 64 to 128, with exactly 128 in some layer; column 1 is the kept latitude wavenumbers of each sign, from 32 to 64, with exactly 64 in some layer.
All inputs are finite; a program needn't handle non-finite values.
Results may differ from a plain program's by a relative error of at most 0.001.
Values may be sent and summed in bfloat16 or wider, within the bound.
A program may use at most 128 MiB of HBM per device.

v0:
```python
import math

import jax
import jax.numpy as jnp
from jax import lax
from jax.sharding import PartitionSpec as P

LAT = 256
LON = 512
KEEP_LON = 128
KEEP_LAT = 64


HIGHEST = lax.Precision.HIGHEST


def from_behind(block, axis, distance):
    devices = range(lax.axis_size(axis))
    route = [(i - distance, i) for i in devices if i - distance in devices]
    return lax.ppermute(block, axis, route)


def lon_tables(length, count):
    column = jnp.arange(length, dtype=jnp.int32)
    number = jnp.arange(count, dtype=jnp.int32)
    phase = column[:, None] * number[None, :] % length
    angle = phase.astype(jnp.float32) * (2.0 * math.pi / length)
    factor = 1.0 / math.sqrt(length)
    return (jnp.cos(angle) * factor, jnp.sin(angle) * factor)


def lat_tables(length, half):
    signed = jnp.arange(2 * half, dtype=jnp.int32) - half
    row_index = jnp.arange(length, dtype=jnp.int32)
    phase = signed[:, None] * row_index[None, :] % length
    angle = phase.astype(jnp.float32) * (2.0 * math.pi / length)
    factor = 1.0 / math.sqrt(length)
    return (jnp.cos(angle) * factor, jnp.sin(angle) * factor)


def lat_columns(field, cos_table, sin_table):
    values = field.astype(jnp.float32)
    real_part = jnp.einsum("fl,ibln->ibfn", cos_table, values, precision=HIGHEST)
    imag_part = -jnp.einsum("fl,ibln->ibfn", sin_table, values, precision=HIGHEST)
    return jnp.stack([real_part, imag_part])


def lon_complex(spectrum, cos_table, sin_table):

    def apply(values, table):
        return jnp.einsum("ibfn,nk->ibfk", values, table, precision=HIGHEST)

    real_part = apply(spectrum[0], cos_table) + apply(spectrum[1], sin_table)
    imag_part = apply(spectrum[1], cos_table) - apply(spectrum[0], sin_table)
    return jnp.stack([real_part, imag_part])


def lon_complex_inverse(spectrum, cos_table, sin_table):

    def apply(values, table):
        return jnp.einsum("ibfk,nk->ibfn", values, table, precision=HIGHEST)

    real_part = apply(spectrum[0], cos_table) - apply(spectrum[1], sin_table)
    imag_part = apply(spectrum[1], cos_table) + apply(spectrum[0], sin_table)
    return jnp.stack([real_part, imag_part])


def lat_real_inverse(spectrum, cos_table, sin_table):
    first = jnp.einsum("fl,ibfn->ibln", cos_table, spectrum[0], precision=HIGHEST)
    second = jnp.einsum("fl,ibfn->ibln", sin_table, spectrum[1], precision=HIGHEST)
    return first - second


def mode_mask(signed, wavenumber, keep_lon, keep_lat):
    lat_kept = (signed >= -keep_lat) & (signed < keep_lat)
    lon_kept = wavenumber < keep_lon
    factor = jnp.where(wavenumber == 0, 1.0, 2.0).astype(jnp.float32)
    return (lat_kept[:, None] & lon_kept[None, :]).astype(jnp.float32) * factor[None, :]


def block_product(weights, values):
    return jnp.einsum("kij,kjm->kim", weights, values, precision=HIGHEST)


def complex_apply(weights, values):
    real_part = block_product(weights[0], values[0]) - block_product(weights[1], values[1])
    imag_part = block_product(weights[1], values[0]) + block_product(weights[0], values[1])
    return jnp.stack([real_part, imag_part])


def complex_adjoint(weights, values):
    real_t = jnp.swapaxes(weights[0], 1, 2)
    imag_t = jnp.swapaxes(weights[1], 1, 2)
    real_part = block_product(real_t, values[0]) + block_product(imag_t, values[1])
    imag_part = block_product(real_t, values[1]) - block_product(imag_t, values[0])
    return jnp.stack([real_part, imag_part])


def complex_outer(left, right):

    def outer(first, second):
        return jnp.einsum("kim,kjm->kij", first, second, precision=HIGHEST)

    real_part = outer(left[0], right[0]) + outer(left[1], right[1])
    imag_part = outer(left[1], right[0]) - outer(left[0], right[1])
    return jnp.stack([real_part, imag_part])


def gelu_pair(values):
    inner = 0.7978845608 * (values + 0.044715 * values * values * values)
    tangent = jnp.tanh(inner)
    output = 0.5 * values * (1.0 + tangent)
    slope = 0.5 * (1.0 + tangent) + 0.5 * values * (1.0 - tangent * tangent) * 0.7978845608 * (
        1.0 + 3.0 * 0.044715 * values * values
    )
    return (output, slope)


def backprop(spectrum, grad_spec, weight_in, bias_in, weight_out):
    before = complex_apply(weight_in, spectrum) + bias_in[..., None]
    hidden, slope = gelu_pair(before)
    grad_hidden = complex_adjoint(weight_out, grad_spec)
    grad_before = grad_hidden * slope
    grad_modes = complex_adjoint(weight_in, grad_before)
    grad_w_out = complex_outer(grad_spec, hidden)
    grad_w_in = complex_outer(grad_before, spectrum)
    return (
        grad_modes,
        grad_w_in,
        jnp.sum(grad_before, axis=-1),
        grad_w_out,
        jnp.sum(grad_spec, axis=-1),
    )


def shards(activations, cotangent, kept_modes, weight_in, bias_in, weight_out):
    field = activations[0]
    own_grad = cotangent[0]
    nblocks = field.shape[0]
    width = field.shape[1]
    received = from_behind(own_grad, "pipe", -1)
    section_index = lax.axis_index("pipe")
    last_section = lax.axis_size("pipe") - 1
    upstream = jnp.where(section_index == last_section, own_grad, received)
    lon_cos, lon_sin = lon_tables(LON, KEEP_LON)
    lat_cos, lat_sin = lat_tables(LAT, KEEP_LAT)
    col_field, col_grad = (
        lax.all_to_all(field, "space", split_axis=3, concat_axis=2, tiled=True),
        lax.all_to_all(upstream, "space", split_axis=3, concat_axis=2, tiled=True),
    )
    lat_field = lat_columns(col_field, lat_cos, lat_sin)
    lat_grad = lat_columns(col_grad, lat_cos, lat_sin)
    part_field, part_grad = (
        lax.all_to_all(lat_field, "space", split_axis=3, concat_axis=4, tiled=True),
        lax.all_to_all(lat_grad, "space", split_axis=3, concat_axis=4, tiled=True),
    )
    share = 2 * KEEP_LAT // lax.axis_size("space")
    signed = lax.axis_index("space") * share + jnp.arange(share, dtype=jnp.int32) - KEEP_LAT
    wavenumber = jnp.arange(KEEP_LON, dtype=jnp.int32)
    weight = mode_mask(signed, wavenumber, kept_modes[0, 0], kept_modes[0, 1])
    spectrum = lon_complex(part_field, lon_cos, lon_sin).reshape(2, nblocks, width, -1)
    grad_spec = (lon_complex(part_grad, lon_cos, lon_sin) * weight).reshape(2, nblocks, width, -1)
    grad_modes, grad_w_in, grad_b_in, grad_w_out, grad_b_out = backprop(
        spectrum, grad_spec, weight_in[0], bias_in[0], weight_out[0]
    )
    grad_modes = grad_modes.reshape(2, nblocks, width, share, KEEP_LON)
    lon_back = lon_complex_inverse(grad_modes, lon_cos, lon_sin)
    lat_parts = lax.all_to_all(lon_back, "space", split_axis=4, concat_axis=3, tiled=True)
    cols_back = lat_real_inverse(lat_parts, lat_cos, lat_sin)
    inverse = lax.all_to_all(cols_back, "space", split_axis=2, concat_axis=3, tiled=True)
    sum_w_in, sum_b_in, sum_w_out, sum_b_out = lax.psum(
        (grad_w_in, grad_b_in, grad_w_out, grad_b_out), "space"
    )
    factor = 1.0 / math.sqrt(2 * KEEP_LAT * KEEP_LON)
    grad_field = (upstream.astype(jnp.float32) + inverse).astype(jnp.bfloat16)
    return (
        grad_field[None],
        (sum_w_in * factor)[None],
        (sum_b_in * factor)[None],
        (sum_w_out * factor)[None],
        (sum_b_out * factor)[None],
    )


def solution(mesh):
    return jax.shard_map(
        shards,
        mesh=mesh,
        in_specs=(
            P("pipe", None, None, "space", None),
            P("pipe", None, None, "space", None),
            P("pipe", None),
            P("pipe", None, None, None, None),
            P("pipe", None, None, None),
            P("pipe", None, None, None, None),
        ),
        out_specs=(
            P("pipe", None, None, "space", None),
            P("pipe", None, None, None, None),
            P("pipe", None, None, None),
            P("pipe", None, None, None, None),
            P("pipe", None, None, None),
        ),
        check_vma=False,
    )
```

profile of v0, /device:TPU:0, one launch (start us, length us, event | category | flops | bytes accessed | tf_op | source)
XLA Modules:
  0.0 1165.3 jit_solution(10960498103045936025)
XLA Ops:
  7.2 8.5 copy.178
  15.7 7.7 all-to-all-start.2
  30.0 65.7 %collective-permute-done = bf16[2,96,16,512]{3,2,1,0:T(8,128)(2,1)} collective-permute-done((bf16[2,96,16,512]{3,2,1,0:T(8,128)(2,1)S(1)}, bf16[2,96,16,512]{3,2,1,0:T(8,128)(2,1)}, u32[]{:S(2)}, u32[]{:S(2)}) %collective-permute-start) | collective-permute-done | bytes 3145760 | tf_op jit(solution)/shard_map/ppermute | solution.py:20
  95.7 7.5 copy.160
  142.0 9.5 copy.183
  151.5 47.1 %all-to-all-done = bf16[2,96,16,512]{1,2,0,3:T(8,128)(2,1)} async-done(((bf16[2,96,16,512]{1,2,0,3:T(8,128)(2,1)}), bf16[2,96,16,512]{1,2,0,3:T(8,128)(2,1)}, u32[]{:S(2)}, u32[]{:S(2)}) %all-to-all-start) | async-done | bytes 3145760 | tf_op jit(solution)/shard_map/all_to_all | solution.py:149
  198.6 19.9 %all-to-all-start.3 = ((f32[2,2,96,128,32]{2,4,1,0,3:T(8,128)}), f32[2,2,96,128,32]{2,4,1,0,3:T(8,128)}, u32[]{:S(2)}, u32[]{:S(2)}) async-start(f32[2,2,96,128,32]{2,4,1,0,3:T(8,128)} %copy.183), calls=%async_computation.3 | async-start | bytes 16777216 | tf_op jit(solution)/shard_map/all_to_all | solution.py:154
  241.1 10.1 copy.166
  251.1 118.0 %all-to-all-done.3 = f32[2,2,96,128,32]{2,4,1,0,3:T(8,128)} async-done(((f32[2,2,96,128,32]{2,4,1,0,3:T(8,128)}), f32[2,2,96,128,32]{2,4,1,0,3:T(8,128)}, u32[]{:S(2)}, u32[]{:S(2)}) %all-to-all-start.3) | async-done | bytes 6291488 | tf_op jit(solution)/shard_map/all_to_all | solution.py:154
  369.2 36.9 %all-to-all-start.1 = ((f32[2,2,96,128,32]{2,4,1,0,3:T(8,128)}), f32[2,2,96,128,32]{2,4,1,0,3:T(8,128)}, u32[]{:S(2)}, u32[]{:S(2)}) async-start(f32[2,2,96,128,32]{2,4,1,0,3:T(8,128)} %copy.166), calls=%async_computation.1 | async-start | bytes 16777216 | tf_op jit(solution)/shard_map/all_to_all | solution.py:155
  416.0 7.6 fusion.61
  423.5 7.7 fusion.13
  432.1 7.8 fusion.59
  451.7 104.7 %all-to-all-done.1 = f32[2,2,96,128,32]{2,4,1,0,3:T(8,128)} async-done(((f32[2,2,96,128,32]{2,4,1,0,3:T(8,128)}), f32[2,2,96,128,32]{2,4,1,0,3:T(8,128)}, u32[]{:S(2)}, u32[]{:S(2)}) %all-to-all-start.1) | async-done | bytes 6291488 | tf_op jit(solution)/shard_map/all_to_all | solution.py:155
  571.5 7.7 fusion.63
  579.2 7.5 convolution_add_fusion.4
  586.8 7.8 convolution_subtract_fusion.4
  624.7 9.7 copy.197
  634.4 218.8 %all_to_all.99 = f32[2,2,96,8,512]{2,3,1,0,4:T(8,128)S(1)} all-to-all(f32[2,2,96,8,512]{2,3,1,0,4:T(8,128)} %copy.197), channel_id=1, replica_groups=mesh['pipe'=2,'space'=16] {'space'}, dimensions={4} | all-to-all | bytes 12582912 | tf_op jit(solution)/shard_map/all_to_all | solution.py:168
  880.0 7.6 fusion.76
  887.6 8.0 subtract_bitcast_fusion
  895.7 10.2 copy.203
  932.2 148.4 %all-reduce = (f32[2,2,96]{2,1,0:T(2,128)S(1)}, f32[2,2,96]{2,1,0:T(2,128)S(1)}) all-reduce(f32[2,2,96]{2,1,0:T(2,128)S(1)} %get-tuple-element.29, f32[2,2,96]{2,1,0:T(2,128)S(1)} %fusion.7), channel_id=1, replica_groups=mesh['pipe'=2,'space'=16] {'space'}, use_global_device_ids=true, to_apply=%region_2.3 | all-reduce | flops 768 | bytes 6144 | tf_op jit(solution)/shard_map/psum | solution.py:171
  1081.2 59.8 %all-reduce.4.cloned.1.call-done = (f32[2,2,96,96]{3,2,1,0:T(8,128)}, f32[2,2,96,96]{3,2,1,0:T(8,128)}) async-done(((f32[2,2,96,96]{3,2,1,0:T(8,128)}, f32[2,2,96,96]{3,2,1,0:T(8,128)}), (f32[2,2,96,96]{3,2,1,0:T(8,128)}, f32[2,2,96,96]{3,2,1,0:T(8,128)})) %all-reduce.4.cloned.1.call-update) | async-done | bytes 294928 | tf_op jit(solution)/shard_map/psum | solution.py:171
  (127 shorter events, 205.4 us)
Async XLA Ops:
  15.6 7.7 copy-start.11
  15.7 98.2 %all-to-all-start.2 = ((bf16[2,96,16,512]{1,2,0,3:T(8,128)(2,1)}), bf16[2,96,16,512]{1,2,0,3:T(8,128)(2,1)}, u32[]{:S(2)}, u32[]{:S(2)}) async-start(bf16[2,96,16,512]{1,2,0,3:T(8,128)(2,1)} %bitcast.291), calls=%async_computation.2 | async-start | bytes 8388608 | tf_op jit(solution)/shard_map/all_to_all | solution.py:148
  23.4 72.4 %collective-permute-start = (bf16[2,96,16,512]{3,2,1,0:T(8,128)(2,1)S(1)}, bf16[2,96,16,512]{3,2,1,0:T(8,128)(2,1)}, u32[]{:S(2)}, u32[]{:S(2)}) collective-permute-start(bf16[2,96,16,512]{3,2,1,0:T(8,128)(2,1)S(1)} %bitcast.303), channel_id=1, source_target_pairs={{16,0},{17,1},{18,2},{19,3},{20,4},{21,5},{22,6},{23,7},{24,8},{25... | collective-permute-start | bytes 9437192 | tf_op jit(solution)/shard_map/ppermute | solution.py:20
  107.2 1.9 copy-start
  113.8 84.7 %all-to-all-start = ((bf16[2,96,16,512]{1,2,0,3:T(8,128)(2,1)}), bf16[2,96,16,512]{1,2,0,3:T(8,128)(2,1)}, u32[]{:S(2)}, u32[]{:S(2)}) async-start(bf16[2,96,16,512]{1,2,0,3:T(8,128)(2,1)} %copy.161), calls=%async_computation | async-start | bytes 8388608 | tf_op jit(solution)/shard_map/all_to_all | solution.py:149
  198.6 170.6 %all-to-all-start.3 = ((f32[2,2,96,128,32]{2,4,1,0,3:T(8,128)}), f32[2,2,96,128,32]{2,4,1,0,3:T(8,128)}, u32[]{:S(2)}, u32[]{:S(2)}) async-start(f32[2,2,96,128,32]{2,4,1,0,3:T(8,128)} %copy.183), calls=%async_computation.3 | async-start | bytes 16777216 | tf_op jit(solution)/shard_map/all_to_all | solution.py:154
  251.1 155.0 %copy-start.18 = (s32[1,2]{1,0:T(1,128)S(1)}, s32[1,2]{1,0:T(1,128)}, u32[]{:S(2)}) copy-start(s32[1,2]{1,0:T(1,128)} %param.8) | copy-start | bytes 28
  369.2 187.3 %all-to-all-start.1 = ((f32[2,2,96,128,32]{2,4,1,0,3:T(8,128)}), f32[2,2,96,128,32]{2,4,1,0,3:T(8,128)}, u32[]{:S(2)}, u32[]{:S(2)}) async-start(f32[2,2,96,128,32]{2,4,1,0,3:T(8,128)} %copy.166), calls=%async_computation.1 | async-start | bytes 16777216 | tf_op jit(solution)/shard_map/all_to_all | solution.py:155
  423.5 7.8 copy-start.10
  431.3 17.9 %copy-start.2 = (f32[2,8,12,8,128]{4,3,2,1,0:T(8,128)}, f32[2,8,12,8,128]{4,3,2,1,0:T(8,128)S(1)}, u32[]{:S(2)}) copy-start(f32[2,8,12,8,128]{4,3,2,1,0:T(8,128)S(1)} %fusion.13) | copy-start | bytes 2359300
  447.4 2.6 copy-start.4
  586.8 7.9 copy-start.8
  597.4 2.6 copy-start.14
  597.4 2.6 copy-start.15
  597.5 2.6 copy-start.17
  880.0 7.6 copy-start.7
  905.9 236.9 %all-to-all-start.5 = ((f32[2,96,256,32]{1,3,0,2:T(8,128)}), f32[2,96,256,32]{1,3,0,2:T(8,128)}, u32[]{:S(2)}, u32[]{:S(2)}) async-start(f32[2,96,256,32]{1,3,0,2:T(8,128)} %copy.203), calls=%async_computation.5 | async-start | bytes 16777216 | tf_op jit(solution)/shard_map/all_to_all | solution.py:170
  911.6 229.4 %all-reduce.4.cloned.1.call-start = ((), (), s32[]{:S(2)}) async-start(), calls=%async_computation.6 | async-start | bytes 786432 | tf_op jit(solution)/shard_map/psum | solution.py:171
  921.1 4.2 copy-start.6
  923.2 4.5 copy-start.3
  925.3 3.3 copy-start.5
  928.6 3.3 copy-start.12
  928.6 3.3 copy-start.13
  1142.8 5.0 copy-start.1
  (2 other events, 2.1 us)
Sparse Core Ops, SparseCore 0:
  932.1 208.8 all-reduce.3
where the time goes:
time: 1170 us
  waiting for transfers between devices  395 us (34%)
  blocking collectives  367 us (31%)
  local copies, waits for them, and re-layouts  158 us (14%)
  matrix products  125 us (11%)
  starting transfers between devices  78.9 us (7%)
  other arithmetic  25.3 us (2%)
  between operations  15.6 us (1%)
    all_to_all x1, blocking collectives, shards(): lax.all_to_all(lon_back, 'space', split_axis=4, concat_axis=3, tiled=True)  219 us
    psum x1, blocking collectives, shards(): lax.psum((grad_w_in, grad_b_in, grad_w_out, grad_b_out), 'space')  148 us
    all_to_all x1, waiting for transfers between devices, shards(): lax.all_to_all(lat_field, 'space', split_axis=3, concat_axis=4, tiled=True)  118 us
    all_to_all x1, waiting for transfers between devices, shards(): lax.all_to_all(lat_grad, 'space', split_axis=3, concat_axis=4, tiled=True)  105 us
    ppermute x1, waiting for transfers between devices, from_behind(): return lax.ppermute(block, axis, route)  65.7 us
    dot_general x8, matrix products, apply(): return jnp.einsum('ibfn,nk->ibfk', values, table, precision=HIGHEST)  61.1 us
    psum x1, waiting for transfers between devices, shards(): lax.psum((grad_w_in, grad_b_in, grad_w_out, grad_b_out), 'space')  59.8 us
    all_to_all x1, waiting for transfers between devices, shards(): lax.all_to_all(upstream, 'space', split_axis=3, concat_axis=2, tiled=True)  47.1 us
  transfers between devices with their start and end apart: 7, of which 5 were waited for; matrix products, arithmetic and copies ran while one was open for 13% of the time, Pallas kernels for 0%

commit v1 on v0

v1 whole, which is shorter than its diff:
```python
import math

import jax
import jax.numpy as jnp
import numpy as np
from jax import lax
from jax.sharding import PartitionSpec as P

KEEP_LON = 128
KEEP_LAT = 64
HIGH = lax.Precision.HIGH
F32 = jnp.float32
F16 = jnp.float16


def from_behind(block, axis, distance):
    devices = range(lax.axis_size(axis))
    route = [(i - distance, i) for i in devices if i - distance in devices]
    return lax.ppermute(block, axis, route)


def lon_table(length, ndev):
    number = np.arange(KEEP_LON)[:, None] * np.arange(length)[None, :] % length
    angle = number * (2.0 * math.pi / length)
    table = np.stack([np.cos(angle), -np.sin(angle)]) / math.sqrt(length)
    table = table.reshape(2, ndev, KEEP_LON // ndev, length).transpose(1, 0, 2, 3)
    return table.astype(np.float32)


def lat_table(length):
    signed = np.arange(2 * KEEP_LAT) - KEEP_LAT
    angle = (signed[:, None] * np.arange(length)[None, :] % length) * (2.0 * math.pi / length)
    cos, sin = np.cos(angle) / math.sqrt(length), np.sin(angle) / math.sqrt(length)
    table = np.stack([np.stack([cos, sin], 1), np.stack([-sin, cos], 1)])
    return table.astype(np.float32)


def mode_mask(signed, wavenumber, keep_lon, keep_lat):
    lat_kept = (signed >= -keep_lat) & (signed < keep_lat)
    lon_kept = wavenumber < keep_lon
    factor = jnp.where(wavenumber == 0, 1.0, 2.0).astype(F32)
    return (lat_kept[:, None] & lon_kept[None, :]).astype(F32) * factor[None, :]


def real_form(weights):
    re, im = jnp.swapaxes(weights[0], 1, 2), jnp.swapaxes(weights[1], 1, 2)
    return jnp.stack([jnp.stack([re, im], 2), jnp.stack([-im, re], 2)])


def gelu_pair(values):
    inner = 0.7978845608 * (values + 0.044715 * values * values * values)
    tangent = jnp.tanh(inner)
    output = 0.5 * values * (1.0 + tangent)
    slope = 0.5 * (1.0 + tangent) + 0.5 * values * (1.0 - tangent * tangent) * 0.7978845608 * (
        1.0 + 3.0 * 0.044715 * values * values
    )
    return (output, slope)


def largest(values):
    return jnp.maximum(jnp.max(jnp.abs(values.astype(F32))), 1e-30)


def complex_outer(left, right):
    def outer(first, second):
        return jnp.einsum("mki,mkj->kij", first, second, precision=HIGH)

    real_part = outer(left[0], right[0]) + outer(left[1], right[1])
    imag_part = outer(left[1], right[0]) - outer(left[0], right[1])
    return jnp.stack([real_part, imag_part])


def shards(activations, cotangent, kept_modes, weight_in, bias_in, weight_out):
    field = activations[0]
    own_grad = cotangent[0]
    nblocks, width, rows, lon = field.shape
    channels = nblocks * width
    ndev = lax.axis_size("space")
    npipe = lax.axis_size("pipe")
    lat = rows * ndev
    share = KEEP_LON // ndev
    section = lax.axis_index("pipe")
    received = from_behind(own_grad, "pipe", -1)
    upstream = jnp.where(section == npipe - 1, own_grad, received)

    peaks = lax.all_gather(
        jnp.stack([largest(field), largest(own_grad)]), ("pipe", "space")
    ).reshape(npipe, ndev, 2)
    source = jnp.minimum(section + 1, npipe - 1)
    place = lax.axis_index("space")
    field_peaks = lax.dynamic_index_in_dim(peaks[:, :, 0], section, 0, False)
    grad_peaks = lax.dynamic_index_in_dim(peaks[:, :, 1], source, 0, False)

    lon_forward = jnp.asarray(lon_table(lon, ndev))
    lat_forward = jnp.asarray(lat_table(lat))

    def transform(values, peak, peaks_all):
        rows_first = jnp.swapaxes(values.reshape(channels, rows, lon), 0, 1)
        spectrum = jnp.einsum(
            "dpkn,lcn->dpklc", lon_forward, rows_first.astype(F32), precision=HIGH
        )
        sent = (spectrum * (1024.0 / peak)).astype(F16)
        got = lax.all_to_all(sent, "space", split_axis=0, concat_axis=0, tiled=True)
        table = lat_forward.reshape(2, 2 * KEEP_LAT, 2, ndev, rows)
        table = table * (peaks_all * (1.0 / 1024.0))[:, None]
        got = got.astype(F32)
        return jnp.einsum("qfpsl,spklc->qfkc", table, got, precision=HIGH)

    spec_field = transform(field, lax.dynamic_index_in_dim(field_peaks, place, 0, False), field_peaks)
    spec_grad = transform(upstream, lax.dynamic_index_in_dim(grad_peaks, place, 0, False), grad_peaks)

    signed = jnp.arange(2 * KEEP_LAT, dtype=jnp.int32) - KEEP_LAT
    wavenumber = place * share + jnp.arange(share, dtype=jnp.int32)
    mask = mode_mask(signed, wavenumber, kept_modes[0, 0], kept_modes[0, 1])
    modes = 2 * KEEP_LAT * share
    z = spec_field.reshape(2, modes, nblocks, width)
    g = (spec_grad * mask[:, :, None]).reshape(2, modes, nblocks, width)

    map_in, map_out = real_form(weight_in[0]), real_form(weight_out[0])
    before = jnp.einsum("pmkj,pkjqi->qmki", z, map_in, precision=HIGH) + bias_in[0][:, None]
    hidden, slope = gelu_pair(before)
    grad_hidden = jnp.einsum("qmki,pkjqi->pmkj", g, map_out, precision=HIGH)
    grad_before = grad_hidden * slope
    grad_modes = jnp.einsum("qmki,pkjqi->pmkj", grad_before, map_in, precision=HIGH)
    grads = (
        complex_outer(grad_before, z),
        jnp.sum(grad_before, axis=1),
        complex_outer(g, hidden),
        jnp.sum(g, axis=1),
    )

    peak = largest(grad_modes)
    back_peaks = lax.all_gather(peak, "space")
    grad_modes = grad_modes.reshape(2, 2 * KEEP_LAT, share, channels)
    lat_back = jnp.einsum(
        "qfpsl,qfkc->spklc",
        lat_forward.reshape(2, 2 * KEEP_LAT, 2, ndev, rows),
        grad_modes,
        precision=HIGH,
    )
    sent = (lat_back * (4000.0 / peak)).astype(F16)
    got = lax.all_to_all(sent, "space", split_axis=0, concat_axis=0, tiled=True).astype(F32)
    lon_back = lon_forward * (back_peaks * (1.0 / 4000.0))[:, None, None, None]
    inverse = jnp.einsum("dpkn,dpklc->lcn", lon_back, got, precision=HIGH)
    inverse = jnp.swapaxes(inverse, 0, 1).reshape(nblocks, width, rows, lon)
    grad_field = (upstream.astype(F32) + inverse).astype(jnp.bfloat16)

    sums = lax.psum(grads, "space")
    factor = 1.0 / math.sqrt(2 * KEEP_LAT * KEEP_LON)
    return (grad_field[None],) + tuple((s * factor)[None] for s in sums)


def solution(mesh):
    return jax.shard_map(
        shards,
        mesh=mesh,
        in_specs=(
            P("pipe", None, None, "space", None),
            P("pipe", None, None, "space", None),
            P("pipe", None),
            P("pipe", None, None, None, None),
            P("pipe", None, None, None),
            P("pipe", None, None, None, None),
        ),
        out_specs=(
            P("pipe", None, None, "space", None),
            P("pipe", None, None, None, None),
            P("pipe", None, None, None),
            P("pipe", None, None, None, None),
            P("pipe", None, None, None),
        ),
        check_vma=False,
    )
```

time: 1170 us -> 471 us (0.40)
  waiting for transfers between devices: 395 us -> 128 us
  blocking collectives: 367 us -> 163 us
  local copies, waits for them, and re-layouts: 158 us -> 59.1 us
  matrix products: 125 us -> 44.8 us
  starting transfers between devices: 78.9 us -> 29.7 us
    all_to_all x5 -> x3, waiting for transfers between devices: 270 us -> 33.6 us  [the longest x2 33.6 us: transform(): got = lax.all_to_all(sent, 'space', split_axis=0, concat_axis=0, tiled=True)]
    all_to_all x1 -> x0, blocking collectives: 219 us -> none  [shards(): lax.all_to_all(lon_back, 'space', split_axis=4, concat_axis=3, tiled=True)]
    unnamed x0 -> x2, blocking collectives: none -> 163 us
    psum x1 -> x0, blocking collectives: 148 us -> none  [shards(): lax.psum((grad_w_in, grad_b_in, grad_w_out, grad_b_out), 'space')]
    dot_general x38 -> x17, matrix products: 125 us -> 44.8 us  [the longest x2 11.4 us: transform(): return jnp.einsum('qfpsl,spklc->qfkc', table, got, precision=HIGH)]
    ppermute x1, waiting for transfers between devices: 65.7 us -> 0.01 us  [from_behind(): return lax.ppermute(block, axis, route)]
    all_to_all x5 -> x3, starting transfers between devices: 77.4 us -> 28.1 us  [the longest x2 16.7 us: transform(): got = lax.all_to_all(sent, 'space', split_axis=0, concat_axis=0, tiled=True)]
    all_to_all x8 -> x0, local copies, waits for them, and re-layouts: 43 us -> none  [the longest x2 12.8 us: shards(): lax.all_to_all(upstream, 'space', split_axis=3, concat_axis=2, tiled=True)]
  transfers between devices with their start and end apart: 7 -> 5, of which waited for: 5 -> 3; matrix products, arithmetic and copies ran while one was open for 13% -> 18% of each run, Pallas kernels for 0% -> 0%
where the time goes in v1:
time: 471 us; the launch traced here: 463 us
  blocking collectives  163 us (35%)
  waiting for transfers between devices  128 us (27%)
  local copies, waits for them, and re-layouts  59.1 us (13%)
  matrix products  44.8 us (10%)
  starting transfers between devices  29.7 us (6%)
  other arithmetic  21.5 us (5%)
  between operations  17.4 us (4%)
    unnamed x2, blocking collectives  163 us
    psum x1, waiting for transfers between devices, shards(): sums = lax.psum(grads, 'space')  94.1 us
    all_to_all x2, waiting for transfers between devices, transform(): got = lax.all_to_all(sent, 'space', split_axis=0, concat_axis=0, tiled=True)  33.6 us
    squeeze x8, local copies, waits for them, and re-layouts, complex_outer(): real_part = outer(left[0], right[0]) + outer(left[1], right[1])  17.1 us
    all_to_all x2, starting transfers between devices, transform(): got = lax.all_to_all(sent, 'space', split_axis=0, concat_axis=0, tiled=True)  16.7 us
    all_to_all x1, starting transfers between devices, shards(): lax.all_to_all(sent, 'space', split_axis=0, concat_axis=0, tiled=True)  11.4 us
    dot_general x2, matrix products, transform(): return jnp.einsum('qfpsl,spklc->qfkc', table, got, precision=HIGH)  11.4 us
    dot_general x2, matrix products, transform(): jnp.einsum('dpkn,lcn->dpklc', lon_forward, rows_first.astype(F32), precis...  10.8 us
  transfers between devices with their start and end apart: 5, of which 3 were waited for; matrix products, arithmetic and copies ran while one was open for 18% of the time, Pallas kernels for 0%

profile of v1, /device:TPU:0, one launch (start us, length us, event | category | flops | bytes accessed | tf_op | source)
XLA Modules:
  0.0 463.0 jit_solution(9024329661815627360)
XLA Ops:
  8.7 3.2 abs_reduce_fusion.1
  14.7 100.7 %all-reduce = f32[64]{0:T(128)S(1)} all-reduce(f32[64]{0:T(128)S(1)} %maximum_dynamic-update-slice_fusion), channel_id=2, replica_groups=mesh['pipe'=2,'space'=16] {'pipe','space'}, use_global_device_ids=true, to_apply=%add | all-reduce | flops 64 | bytes 512
  116.2 6.4 %multiply_convert_fusion = f16[16,2,8,16,192]{4,0,1,3,2:T(8,128)(2,1)S(1)} fusion(f32[]{:T(128)} %bitcast.54, f32[16,2,8,512,1]{3,0,1,4,2:T(8,128)} %constant.123, bf16[192,16,512]{2,1,0:T(8,128)(2,1)} %bitcast.215), kind=kOutput, calls=%fused_computation.6 | convolution fusion | flops 2417491968 | bytes 5242884 | tf_op jit(solution)/shard_map/dpkn,lcn->dpklc/dot_general | solution.py:99
  122.5 4.1 copy.100
  126.6 5.3 %all-to-all-start.1 = ((f16[16,2,8,16,192]{4,1,3,2,0:T(2,128)(2,1)}), f16[16,2,8,16,192]{4,1,3,2,0:T(2,128)(2,1)}, u32[]{:S(2)}, u32[]{:S(2)}) async-start(f16[16,2,8,16,192]{4,1,3,2,0:T(2,128)(2,1)} %copy.100), calls=%async_computation.1 | async-start | bytes 4194304 | tf_op jit(solution)/shard_map/all_to_all | solution.py:103
  136.0 4.4 fusion.9
  140.4 4.0 copy.94
  144.5 28.6 %all-to-all-done.1 = f16[16,2,8,16,192]{4,1,3,2,0:T(2,128)(2,1)} async-done(((f16[16,2,8,16,192]{4,1,3,2,0:T(2,128)(2,1)}), f16[16,2,8,16,192]{4,1,3,2,0:T(2,128)(2,1)}, u32[]{:S(2)}, u32[]{:S(2)}) %all-to-all-start.1) | async-done | bytes 1572896 | tf_op jit(solution)/shard_map/all_to_all | solution.py:103
  173.1 11.5 %all-to-all-start = ((f16[16,2,8,16,192]{4,1,3,2,0:T(2,128)(2,1)}), f16[16,2,8,16,192]{4,1,3,2,0:T(2,128)(2,1)}, u32[]{:S(2)}, u32[]{:S(2)}) async-start(f16[16,2,8,16,192]{4,1,3,2,0:T(2,128)(2,1)} %copy.94), calls=%async_computation | async-start | bytes 4194304 | tf_op jit(solution)/shard_map/all_to_all | solution.py:103
  188.8 5.6 %fusion.13 = f32[2,128,8,192,1,1]{1,3,5,2,0,4:T(8,128)S(1)} fusion(f16[16,2,8,16,192,1]{4,1,3,2,0,5:T(2,128)(2,1)} %bitcast.55, f32[2,128,2,16,16,1]{1,3,0,2,4,5:T(8,128)S(1)} %get-tuple-element.27), kind=kOutput, calls=%fused_computation.22 | convolution fusion | flops 1207959552 | bytes 3670016 | tf_op jit(solution)/shard_map/qfpsl,spklc->qfkc/dot_general | solution.py:107
  205.1 2.9 squeeze.72
  211.6 2.9 squeeze.74
  216.4 4.3 multiply_multiply_fusion.1
  220.7 5.0 %all-to-all-done = f16[16,2,8,16,192]{4,1,3,2,0:T(2,128)(2,1)} async-done(((f16[16,2,8,16,192]{4,1,3,2,0:T(2,128)(2,1)}), f16[16,2,8,16,192]{4,1,3,2,0:T(2,128)(2,1)}, u32[]{:S(2)}, u32[]{:S(2)}) %all-to-all-start) | async-done | bytes 1572896 | tf_op jit(solution)/shard_map/all_to_all | solution.py:103
  225.6 5.7 %fusion.17 = f32[2,128,8,192,1,1]{1,3,5,2,0,4:T(8,128)S(1)} fusion(f16[16,2,8,16,192,1]{4,1,3,2,0,5:T(2,128)(2,1)} %bitcast.40, f32[2,128,2,16,16,1]{1,3,0,2,4,5:T(8,128)S(1)} %get-tuple-element.26), kind=kOutput, calls=%fused_computation.26 | convolution fusion | flops 1207959552 | bytes 3670016 | tf_op jit(solution)/shard_map/qfpsl,spklc->qfkc/dot_general | solution.py:107
  234.9 2.7 reshape.146
  237.6 3.6 fusion.73
  252.2 4.0 copy.109
  256.2 11.4 %all-to-all-start.2 = ((f16[16,2,8,16,192]{4,1,2,3,0:T(2,128)(2,1)}), f16[16,2,8,16,192]{4,1,2,3,0:T(2,128)(2,1)}, u32[]{:S(2)}, u32[]{:S(2)}) async-start(f16[16,2,8,16,192]{4,1,2,3,0:T(2,128)(2,1)} %copy.109), calls=%async_computation.2 | async-start | bytes 4194304 | tf_op jit(solution)/shard_map/all_to_all | solution.py:142
  268.4 62.0 %all-reduce.2 = (f32[16]{0:T(128)S(1)}, f32[2,2,96]{2,0,1:T(2,128)S(1)}, f32[2,2,96]{2,0,1:T(2,128)S(1)}) all-reduce(f32[16]{0:T(128)S(1)} %dynamic-update-slice.1, f32[2,2,96]{2,0,1:T(2,128)S(1)} %get-tuple-element.42, f32[2,2,96]{2,0,1:T(2,128)S(1)} %copy.124), channel_id=1, replica_groups=mesh['pipe'=2,'space'=16] {'space'}, use_global_device_ids=true, to_apply=%add.1 | all-reduce | flops 784 | bytes 6272
  334.5 3.1 squeeze.75
  347.6 94.1 %all-reduce.6.cloned.1.call-done = (f32[2,2,96,96]{3,2,1,0:T(8,128)}, f32[2,2,96,96]{3,2,1,0:T(8,128)}) async-done(((f32[2,2,96,96]{3,2,1,0:T(8,128)}, f32[2,2,96,96]{3,2,1,0:T(8,128)}), (f32[2,2,96,96]{3,2,1,0:T(8,128)}, f32[2,2,96,96]{3,2,1,0:T(8,128)})) %all-reduce.6.cloned.1.call-update) | async-done | bytes 294928 | tf_op jit(solution)/shard_map/psum | solution.py:148
  445.0 5.7 %fusion.19 = f32[16,192,512,1,1]{2,1,4,3,0:T(8,128)S(1)} fusion(f16[16,2,8,16,192]{4,1,2,3,0:T(2,128)(2,1)} %all-to-all-done.2, f32[16,2,8,512]{3,0,1,2:T(8,128)S(1)} %copy-done.21, f32[16]{0:T(128)S(1)} %broadcast_multiply_fusion), kind=kOutput, calls=%fused_computation.28 | convolution fusion | flops 2416050176 | bytes 8388672 | tf_op jit(solution)/shard_map/dpkn,dpklc->lcn/dot_general | solution.py:144
  450.7 5.3 %fusion.2 = bf16[1,2,96,16,512]{4,3,2,1,0:T(8,128)(2,1)} fusion(f32[2,96,16,512]{3,1,0,2:T(8,128)S(1)} %bitcast.213, bf16[2,96,16,512]{3,2,1,0:T(8,128)(2,1)S(1)} %copy-done.5), kind=kLoop, calls=%fused_computation.8 | loop fusion | flops 4718592 | bytes 12582912 | tf_op jit(solution)/shard_map/broadcast_in_dim | solution.py:150
  (119 shorter events, 59.1 us)
Async XLA Ops:
  7.2 5.4 %copy-start.3 = (bf16[1,2,96,16,512]{4,3,2,1,0:T(8,128)(2,1)S(1)}, bf16[1,2,96,16,512]{4,3,2,1,0:T(8,128)(2,1)}, u32[]{:S(2)}) copy-start(bf16[1,2,96,16,512]{4,3,2,1,0:T(8,128)(2,1)} %param.9) | copy-start | bytes 9437188
  7.2 126.5 %collective-permute-start = (bf16[2,96,16,512]{3,2,1,0:T(8,128)(2,1)}, bf16[2,96,16,512]{3,2,1,0:T(8,128)(2,1)}, u32[]{:S(2)}, u32[]{:S(2)}) collective-permute-start(bf16[2,96,16,512]{3,2,1,0:T(8,128)(2,1)} %bitcast.210), channel_id=1, source_target_pairs={{16,0},{17,1},{18,2},{19,3},{20,4},{21,5},{22,6},{23,7},{24,8},{25... | collective-permute-start | bytes 9437192 | tf_op jit(solution)/shard_map/ppermute | solution.py:19
  126.6 5.3 %copy-start.20 = (s32[1,2]{1,0:T(1,128)S(1)}, s32[1,2]{1,0:T(1,128)}, u32[]{:S(2)}) copy-start(s32[1,2]{1,0:T(1,128)} %param.10) | copy-start | bytes 28
  126.6 6.5 %copy-start.19 = (f32[1,2,2,96]{3,2,1,0:T(2,128)S(1)}, f32[1,2,2,96]{3,2,1,0:T(2,128)}, u32[]{:S(2)}) copy-start(f32[1,2,2,96]{3,2,1,0:T(2,128)} %param.12) | copy-start | bytes 4612
  126.6 46.4 %all-to-all-start.1 = ((f16[16,2,8,16,192]{4,1,3,2,0:T(2,128)(2,1)}), f16[16,2,8,16,192]{4,1,3,2,0:T(2,128)(2,1)}, u32[]{:S(2)}, u32[]{:S(2)}) async-start(f16[16,2,8,16,192]{4,1,3,2,0:T(2,128)(2,1)} %copy.100), calls=%async_computation.1 | async-start | bytes 4194304 | tf_op jit(solution)/shard_map/all_to_all | solution.py:103
  133.7 2.3 copy-start.22
  136.0 4.4 copy-start.4
  144.5 40.1 %copy-start.16 = (f32[1,2,2,96,96]{4,3,2,1,0:T(8,128)S(1)}, f32[1,2,2,96,96]{4,3,2,1,0:T(8,128)}, u32[]{:S(2)}) copy-start(f32[1,2,2,96,96]{4,3,2,1,0:T(8,128)} %param.13) | copy-start | bytes 442372
  144.5 40.3 %copy-start.23 = (u32[32]{0:T(128)S(1)}, u32[32]{0:T(128)}, u32[]{:S(2)}) copy-start(u32[32]{0:T(128)} %constant.119) | copy-start | bytes 388
  144.5 42.4 %copy-start.15 = (f32[1,2,2,96,96]{4,3,2,1,0:T(8,128)S(1)}, f32[1,2,2,96,96]{4,3,2,1,0:T(8,128)}, u32[]{:S(2)}) copy-start(f32[1,2,2,96,96]{4,3,2,1,0:T(8,128)} %param.11) | copy-start | bytes 442372
  173.1 52.6 %all-to-all-start = ((f16[16,2,8,16,192]{4,1,3,2,0:T(2,128)(2,1)}), f16[16,2,8,16,192]{4,1,3,2,0:T(2,128)(2,1)}, u32[]{:S(2)}, u32[]{:S(2)}) async-start(f16[16,2,8,16,192]{4,1,3,2,0:T(2,128)(2,1)} %copy.94), calls=%async_computation | async-start | bytes 4194304 | tf_op jit(solution)/shard_map/all_to_all | solution.py:103
  184.5 4.0 copy-start.14
  234.9 2.7 copy-start.17
  234.9 2.7 copy-start.18
  237.6 4.8 %copy-start.11 = (f32[1,2,96,2,96]{2,4,0,3,1:T(8,128)S(1)}, f32[1,2,96,2,96]{2,4,0,3,1:T(8,128)}, u32[]{:S(2)}) copy-start(f32[1,2,96,2,96]{2,4,0,3,1:T(8,128)} %get-tuple-element.34) | copy-start | bytes 442372
  237.6 4.8 %copy-start.12 = (f32[1,2,96,2,96]{2,4,0,3,1:T(8,128)S(1)}, f32[1,2,96,2,96]{2,4,0,3,1:T(8,128)}, u32[]{:S(2)}) copy-start(f32[1,2,96,2,96]{2,4,0,3,1:T(8,128)} %get-tuple-element.35) | copy-start | bytes 442372
  247.1 2.6 copy-start.13
  256.2 74.3 %copy-start.10 = (f32[1,128,8,192]{1,3,0,2:T(8,128)S(1)}, f32[1,128,8,192]{1,3,0,2:T(8,128)}, u32[]{:S(2)}) copy-start(f32[1,128,8,192]{1,3,0,2:T(8,128)} %get-tuple-element.23) | copy-start | bytes 2359300
  256.2 188.7 %all-to-all-start.2 = ((f16[16,2,8,16,192]{4,1,2,3,0:T(2,128)(2,1)}), f16[16,2,8,16,192]{4,1,2,3,0:T(2,128)(2,1)}, u32[]{:S(2)}, u32[]{:S(2)}) async-start(f16[16,2,8,16,192]{4,1,2,3,0:T(2,128)(2,1)} %copy.109), calls=%async_computation.2 | async-start | bytes 4194304 | tf_op jit(solution)/shard_map/all_to_all | solution.py:142
  267.6 174.1 %all-reduce.6.cloned.1.call-start = ((), (), s32[]{:S(2)}) async-start(), calls=%async_computation.3 | async-start | bytes 786432 | tf_op jit(solution)/shard_map/psum | solution.py:148
  334.5 6.5 %copy-start = (f32[2,1024,2,96]{1,3,0,2:T(8,128)S(1)}, f32[2,1024,2,96]{1,3,0,2:T(8,128)}, u32[]{:S(2)}) copy-start(f32[2,1024,2,96]{1,3,0,2:T(8,128)} %get-tuple-element.44) | copy-start | bytes 4718596
  339.8 2.8 copy-start.7
  345.9 99.1 %copy-start.21 = (f32[16,2,8,512]{3,0,1,2:T(8,128)S(1)}, f32[16,2,8,512]{3,0,1,2:T(8,128)}, u32[]{:S(2)}) copy-start(f32[16,2,8,512]{3,0,1,2:T(8,128)} %constant.104.clone) | copy-start | bytes 1572868
  445.0 5.7 %copy-start.5 = (bf16[2,96,16,512]{3,2,1,0:T(8,128)(2,1)S(1)}, bf16[2,96,16,512]{3,2,1,0:T(8,128)(2,1)}, u32[]{:S(2)}) copy-start(bf16[2,96,16,512]{3,2,1,0:T(8,128)(2,1)} %copy-done.4) | copy-start | bytes 9437188
  (5 other events, 7.2 us)
Sparse Core Ops, SparseCore 0:
  347.7 93.9 all-reduce.5
